TPU v7x, 32 devices: a whole 2x2x4 slice. The times are simulated.
32 devices in a mesh: grp: 2 (over x), gx: 16 (over z, y, core).
Axes of the slice: x: 2, y: 2, z: 4, core: 2. Of those that a mesh axis runs over, the one named last changes fastest.
Arguments:
- probes: float32 [32, 32, 128, 256], P('grp', 'gx'), parts along dimension 0, may hold values from -6 to 6
- kappa: float32 [64, 128, 256], P(('grp', 'gx')), parts along dimension 0, may hold values from 0.04 to 1.45
- delta: float32 [64, 128, 256], P(('grp', 'gx')), parts along dimension 0, may hold values from 0.2 to 1
- sensor_cells: int32 [4096], P(('grp', 'gx')), parts along dimension 0, may hold values from 0 to 1048575, as said below
- sensor_weights: float32 [4096], P(('grp', 'gx')), parts along dimension 0, may hold values from 1 to 8
Outputs:
- diag_estimate: float32 [64, 128, 256], P(('grp', 'gx')), parts along dimension 0
- sensor_grad: float32 [4096], P(('grp', 'gx')), parts along dimension 0
There are 2 independent parts, one for each index of `grp`. A program takes and returns all parts, laid end to end along the dimension named above; each array names one. Nothing has to cross between parts.
Inputs may be any that keep to these rules, and one draw needn't show every extreme that they name: `sensor_cells`: flat row-major indices into the grid. The entries of block k of 128 are distinct cells whose first coordinate lies in [k * 2, (k + 1) * 2); each block holds the first and last cell of its slab.
All inputs are finite; a program needn't handle non-finite values.
Results may differ from a plain program's by a relative error of at most 0.0001.
Values sent between devices are 32-bit elements; how exact they have to be, the bound alone decides.
A program may use at most 128 MiB of HBM per device.

v0:
```python
import jax
import jax.numpy as jnp
from jax import lax
from jax.sharding import PartitionSpec as P


def with_halo(shard, sides, width):
    for axis, dim in sides:
        size, length = (lax.axis_size(axis), shard.shape[dim])
        up = [(i, (i + 1) % size) for i in range(size - 1)]
        down = [(j, i) for i, j in up]
        last = lax.slice_in_dim(shard, length - width, length, axis=dim)
        leading = lax.slice_in_dim(shard, 0, width, axis=dim)
        before = lax.ppermute(last, axis, up)
        after = lax.ppermute(leading, axis, down)
        shard = jnp.concatenate([before, shard, after], axis=dim)
    return shard


def apply_k(vx, kx, dx):
    vp = jnp.pad(vx, ((0, 0), (0, 0), (1, 1), (1, 1)))
    kp = jnp.pad(kx, ((0, 0), (1, 1), (1, 1)))
    vc = vp[:, 1:-1, 1:-1, 1:-1]
    kc = kp[1:-1, 1:-1, 1:-1]
    near = [
        (vp[:, :-2, 1:-1, 1:-1], kp[:-2, 1:-1, 1:-1]),
        (vp[:, 2:, 1:-1, 1:-1], kp[2:, 1:-1, 1:-1]),
        (vp[:, 1:-1, :-2, 1:-1], kp[1:-1, :-2, 1:-1]),
        (vp[:, 1:-1, 2:, 1:-1], kp[1:-1, 2:, 1:-1]),
        (vp[:, 1:-1, 1:-1, :-2], kp[1:-1, 1:-1, :-2]),
        (vp[:, 1:-1, 1:-1, 2:], kp[1:-1, 1:-1, 2:]),
    ]
    total = dx * vc
    for vn, kn in near:
        total = total + 0.5 * (kc + kn) * (vc - vn)
    return total


def diag_k(kx, dx):
    kp = jnp.pad(kx, ((0, 0), (1, 1), (1, 1)))
    kc = kp[1:-1, 1:-1, 1:-1]
    total = dx
    for kn in [
        kp[:-2, 1:-1, 1:-1],
        kp[2:, 1:-1, 1:-1],
        kp[1:-1, :-2, 1:-1],
        kp[1:-1, 2:, 1:-1],
        kp[1:-1, 1:-1, :-2],
        kp[1:-1, 1:-1, 2:],
    ]:
        total = total + 0.5 * (kc + kn)
    return total


def inner(first, second):
    return jnp.sum(first * second, axis=(1, 2, 3))


def expand(values):
    return values[:, None, None, None]


def shards(probes, kappa, delta, sensor_cells, sensor_weights):
    rows, span_y, span_z = kappa.shape
    cells = rows * span_y * span_z
    place = lax.axis_index("gx")
    local_cells = sensor_cells - place * cells
    obs = (
        jnp.zeros((cells,), jnp.float32)
        .at[local_cells]
        .add(sensor_weights)
        .reshape(rows, span_y, span_z)
    )
    kx_one = with_halo(kappa, (("gx", 0),), 1)

    def rim(field):
        return with_halo(field, (("gx", 1),), 1)

    kdiag = diag_k(kx_one, delta)
    precond = 1.0 / (kdiag * kdiag + obs)
    resid = probes
    precon_res = precond * resid

    def norm_sum(left, right):
        return lax.psum(inner(left, right), "gx")

    solution = jnp.zeros_like(probes)
    gamma = norm_sum(resid, precon_res)
    direction = precon_res
    for step in range(2):
        first = apply_k(rim(direction), kx_one, delta)
        image = apply_k(rim(first), kx_one, delta) + obs * direction
        alpha = gamma / lax.psum(inner(direction, image), "gx")
        solution = solution + expand(alpha) * direction
        resid = resid - expand(alpha) * image
        if step == 0:
            precon_res = precond * resid
            gamma_new = norm_sum(resid, precon_res)
            direction = precon_res + expand(gamma_new / gamma) * direction
            gamma = gamma_new
    diag_estimate = 0.5 * jnp.mean(probes * solution, axis=0)
    sensor_grad = diag_estimate.reshape(-1)[local_cells]
    return (diag_estimate, sensor_grad)


def solution(mesh):
    placed = (
        P("grp", "gx", None, None),
        P(("grp", "gx"), None, None),
        P(("grp", "gx"), None, None),
        P(("grp", "gx")),
        P(("grp", "gx")),
    )
    return jax.shard_map(
        shards,
        mesh=mesh,
        in_specs=placed,
        out_specs=(P(("grp", "gx"), None, None), P(("grp", "gx"))),
        check_vma=False,
    )
```

profile of v0, /device:TPU:0, one launch (start us, length us, event | category | flops | bytes accessed | tf_op | source)
XLA Modules:
  0.0 415.1 jit_solution(13047879873065560029)
XLA Ops:
  1.6 2.4 collective-permute-start
  7.5 1.8 collective-permute-done.1
  10.6 2.3 add_divide_fusion
  13.7 5.6 %collective-permute-start.2 = (f32[16,1,128,256]{3,2,1,0:T(8,128)S(1)}, f32[16,1,128,256]{3,2,1,0:T(8,128)S(1)}, u32[]{:S(2)}, u32[]{:S(2)}) collective-permute-start(f32[16,1,128,256]{3,2,1,0:T(8,128)S(1)} %get-tuple-element.20), channel_id=1, source_target_pairs={{0,1},{1,2},{2,3},{3,4},{4,5},{5,6},{6,7},{7,8},{8,9},{9,10},{10,1... | collective-permute-start | bytes 6291464 | tf_op jit(solution)/shard_map/ppermute | solution.py:14
  20.7 2.2 collective-permute-done.2
  22.9 2.6 collective-permute-done.3
  25.5 7.9 %select_maximum_fusion.6 = f32[16,4,130,258]{3,2,1,0:T(8,128)} fusion(f32[16,1,128,256]{3,2,1,0:T(8,128)S(1)} %collective-permute-done.3, f32[16,2,128,256]{3,2,1,0:T(8,128)S(1)} %broadcast_multiply_fusion, f32[16,1,128,256]{3,2,1,0:T(8,128)S(1)} %collective-permute-done.2), kind=kLoop, calls=%fused_computation.12 | loop fusion | flops 32198400 | bytes 16974848 | tf_op jit(solution)/shard_map/concatenate | solution.py:16
  33.4 13.1 %fusion.51 = f32[16,2,128,256]{3,2,1,0:T(8,128)} fusion(f32[16,2,128,256]{3,2,1,0:T(8,128)S(1)} %broadcast_multiply_fusion, f32[16,4,130,258]{3,2,1,0:T(8,128)} %select_maximum_fusion.6, f32[16,1,128,256]{3,2,1,0:T(8,128)} %copy-done.7, f32[16,1,128,256]{3,2,1,0:T(8,128)S(1)} %collective-permute-done.2, f32[2,128,256]{2,1,0:T(8,128)} %get-tuple-element.13, ...), kind=kLoop, calls=%fused_computation.86 | loop fusion | flops 22020096 | bytes 31195136 | tf_op jit(solution)/shard_map/add | solution.py:35
  46.6 2.7 fusion.86
  49.3 41.2 %collective-permute-start.4 = (f32[16,1,128,256]{3,2,1,0:T(8,128)S(1)}, f32[16,1,128,256]{3,2,1,0:T(8,128)S(1)}, u32[]{:S(2)}, u32[]{:S(2)}) collective-permute-start(f32[16,1,128,256]{3,2,1,0:T(8,128)S(1)} %get-tuple-element.18), channel_id=1, source_target_pairs={{0,1},{1,2},{2,3},{3,4},{4,5},{5,6},{6,7},{7,8},{8,9},{9,10},{10,1... | collective-permute-start | bytes 6291464 | tf_op jit(solution)/shard_map/ppermute | solution.py:14
  92.1 2.2 collective-permute-done.4
  94.2 4.3 %collective-permute-done.5 = f32[16,1,128,256]{3,2,1,0:T(8,128)S(1)} collective-permute-done((f32[16,1,128,256]{3,2,1,0:T(8,128)S(1)}, f32[16,1,128,256]{3,2,1,0:T(8,128)S(1)}, u32[]{:S(2)}, u32[]{:S(2)}) %collective-permute-start.5) | collective-permute-done | bytes 2097184 | tf_op jit(solution)/shard_map/ppermute | solution.py:15
  99.8 7.9 %select_maximum_fusion.4 = f32[16,4,130,258]{3,2,1,0:T(8,128)} fusion(f32[16,1,128,256]{3,2,1,0:T(8,128)S(1)} %collective-permute-done.5, f32[16,2,128,256]{3,2,1,0:T(8,128)S(1)} %copy-done.3, f32[16,1,128,256]{3,2,1,0:T(8,128)S(1)} %collective-permute-done.4), kind=kLoop, calls=%fused_computation.10 | loop fusion | flops 32198400 | bytes 16974848 | tf_op jit(solution)/shard_map/concatenate | solution.py:16
  107.8 17.5 %multiply_reduce_fusion.1 = (f32[16]{0:T(128)S(1)}, f32[16]{0:T(128)S(1)}, f32[16,2,128,256]{3,2,1,0:T(8,128)}) fusion(f32[16,2,128,256]{3,2,1,0:T(8,128)} %param.5, f32[2,128,256]{2,1,0:T(8,128)S(1)} %get-tuple-element.7, f32[2,128,256]{2,1,0:T(8,128)} %copy-done.17, f32[16,2,128,256]{3,2,1,0:T(8,128)} %fusion.51, ...), kind=kLoop, calls=%fused_computation.106 | loop fusion | flops 29360096 | bytes 35913856 | tf_op jit(solution)/shard_map/reduce_sum | solution.py:56
  125.3 69.4 %all-reduce.5 = (f32[16]{0:T(128)S(1)}, f32[16]{0:T(128)S(1)}) all-reduce(f32[16]{0:T(128)S(1)} %get-tuple-element.3, f32[16]{0:T(128)S(1)} %get-tuple-element.2), channel_id=1, replica_groups=mesh['grp'=2,'gx'=16] {'gx'}, use_global_device_ids=true, to_apply=%region_2.3 | all-reduce | flops 32 | bytes 256 | tf_op jit(solution)/shard_map/psum | solution.py:85
  194.7 4.5 %fusion.3 = f32[16]{0:T(128)S(1)} fusion(f32[16,2,128,256]{3,2,1,0:T(8,128)} %param.5, f32[16,2,128,256]{3,2,1,0:T(8,128)} %get-tuple-element.6, f32[16]{0:T(128)S(1)} %div.19, f32[2,128,256]{2,1,0:T(8,128)S(1)} %get-tuple-element.7), kind=kLoop, calls=%fused_computation.19 | loop fusion | flops 5242864 | bytes 8650880 | tf_op jit(solution)/shard_map/reduce_sum | solution.py:56
  199.1 29.5 %psum.30 = f32[16]{0:T(128)S(1)} all-reduce(f32[16]{0:T(128)S(1)} %fusion.3), channel_id=1, replica_groups=mesh['grp'=2,'gx'=16] {'gx'}, use_global_device_ids=true, to_apply=%region_6.7 | all-reduce | flops 16 | bytes 128 | tf_op jit(solution)/shard_map/psum | solution.py:85
  228.6 4.5 %multiply_add_fusion = f32[16,2,128,256]{3,2,1,0:T(8,128)S(1)} fusion(f32[16,2,128,256]{3,2,1,0:T(8,128)} %param.5, f32[16]{0:T(128)S(1)} %div.20, f32[16,2,128,256]{3,2,1,0:T(8,128)} %get-tuple-element.6, f32[16]{0:T(128)S(1)} %div.19, f32[2,128,256]{2,1,0:T(8,128)S(1)} %get-tuple-element.7), kind=kLoop, calls=%fused_computation.17 | loop fusion | flops 6291456 | bytes 12845184 | tf_op jit(solution)/shard_map/add | solution.py:99
  233.6 1.9 collective-permute-start.6
  237.2 1.9 collective-permute-done.6
  239.1 2.6 collective-permute-done.7
  243.1 7.9 %select_maximum_fusion.2 = f32[16,4,130,258]{3,2,1,0:T(8,128)} fusion(f32[16,1,128,256]{3,2,1,0:T(8,128)S(1)} %collective-permute-done.7, f32[16,2,128,256]{3,2,1,0:T(8,128)S(1)} %multiply_add_fusion, f32[16,1,128,256]{3,2,1,0:T(8,128)S(1)} %collective-permute-done.6), kind=kLoop, calls=%fused_computation.8 | loop fusion | flops 32198400 | bytes 16974848 | tf_op jit(solution)/shard_map/concatenate | solution.py:16
  251.0 12.8 %fusion.22 = f32[16,2,128,256]{3,2,1,0:T(8,128)} fusion(f32[16,2,128,256]{3,2,1,0:T(8,128)S(1)} %multiply_add_fusion, f32[16,4,130,258]{3,2,1,0:T(8,128)} %select_maximum_fusion.2, f32[16,1,128,256]{3,2,1,0:T(8,128)} %copy-done.8, f32[16,1,128,256]{3,2,1,0:T(8,128)S(1)} %collective-permute-done.6, f32[2,128,256]{2,1,0:T(8,128)} %get-tuple-element.13, ...), kind=kLoop, calls=%fused_computation.45 | loop fusion | flops 22020096 | bytes 31195136 | tf_op jit(solution)/shard_map/add | solution.py:35
  263.8 2.7 fusion.84
  266.5 41.1 %collective-permute-start.8 = (f32[16,1,128,256]{3,2,1,0:T(8,128)S(1)}, f32[16,1,128,256]{3,2,1,0:T(8,128)S(1)}, u32[]{:S(2)}, u32[]{:S(2)}) collective-permute-start(f32[16,1,128,256]{3,2,1,0:T(8,128)S(1)} %get-tuple-element.14), channel_id=1, source_target_pairs={{0,1},{1,2},{2,3},{3,4},{4,5},{5,6},{6,7},{7,8},{8,9},{9,10},{10,1... | collective-permute-start | bytes 6291464 | tf_op jit(solution)/shard_map/ppermute | solution.py:14
  309.0 2.3 collective-permute-done.8
  311.3 4.3 %collective-permute-done.9 = f32[16,1,128,256]{3,2,1,0:T(8,128)S(1)} collective-permute-done((f32[16,1,128,256]{3,2,1,0:T(8,128)S(1)}, f32[16,1,128,256]{3,2,1,0:T(8,128)S(1)}, u32[]{:S(2)}, u32[]{:S(2)}) %collective-permute-start.9) | collective-permute-done | bytes 2097184 | tf_op jit(solution)/shard_map/ppermute | solution.py:15
  316.9 7.9 %select_maximum_fusion = f32[16,4,130,258]{3,2,1,0:T(8,128)} fusion(f32[16,1,128,256]{3,2,1,0:T(8,128)S(1)} %collective-permute-done.9, f32[16,2,128,256]{3,2,1,0:T(8,128)S(1)} %copy-done.2, f32[16,1,128,256]{3,2,1,0:T(8,128)S(1)} %collective-permute-done.8), kind=kLoop, calls=%fused_computation.6 | loop fusion | flops 32198400 | bytes 16974848 | tf_op jit(solution)/shard_map/concatenate | solution.py:16
  324.9 15.3 %fusion.8 = f32[16]{0:T(128)S(1)} fusion(f32[16,2,128,256]{3,2,1,0:T(8,128)S(1)} %multiply_add_fusion, f32[16,2,128,256]{3,2,1,0:T(8,128)} %fusion.22, f32[16,4,130,258]{3,2,1,0:T(8,128)} %select_maximum_fusion, f32[16,1,128,256]{3,2,1,0:T(8,128)} %copy-done.5, f32[16,1,128,256]{3,2,1,0:T(8,128)} %copy-done.4, f32[2,128,256]{2,1,0:T(8,128)} %copy-done.17, ...), kind=kLoop, calls=%fused_computation.25 | loop fusion | flops 26214384 | bytes 31457344 | tf_op jit(solution)/shard_map/reduce_sum | solution.py:56
  340.2 68.4 %psum.31 = f32[16]{0:T(128)S(1)} all-reduce(f32[16]{0:T(128)S(1)} %fusion.8), channel_id=1, replica_groups=mesh['grp'=2,'gx'=16] {'gx'}, use_global_device_ids=true, to_apply=%region_8.9 | all-reduce | flops 16 | bytes 128 | tf_op jit(solution)/shard_map/psum | solution.py:93
  408.6 4.6 %multiply_reduce_fusion = f32[2,128,256]{2,1,0:T(8,128)S(1)} fusion(f32[16,2,128,256]{3,2,1,0:T(8,128)} %param.5, f32[16,2,128,256]{3,2,1,0:T(8,128)} %copy-done, f32[16]{0:T(128)S(1)} %div.21, f32[16]{0:T(128)S(1)} %div.19, f32[2,128,256]{2,1,0:T(8,128)S(1)} %get-tuple-element.7), kind=kLoop, calls=%fused_computation.104 | loop fusion | flops 6225920 | bytes 8913024 | tf_op jit(solution)/shard_map/reduce_sum | solution.py:101
  413.4 1.7 gather_fusion
  (58 shorter events, 17.1 us)
Async XLA Ops:
  1.6 5.9 %collective-permute-start = (f32[1,128,256]{2,1,0:T(8,128)S(1)}, f32[1,128,256]{2,1,0:T(8,128)S(1)}, u32[]{:S(2)}, u32[]{:S(2)}) collective-permute-start(f32[1,128,256]{2,1,0:T(8,128)S(1)} %get-tuple-element.23), channel_id=1, source_target_pairs={{0,1},{1,2},{2,3},{3,4},{4,5},{5,6},{6,7},{7,8},{8,9},{9,10},{10,1... | collective-permute-start | bytes 393224 | tf_op jit(solution)/shard_map/ppermute | solution.py:14
  4.0 5.4 %collective-permute-start.1 = (f32[1,128,256]{2,1,0:T(8,128)S(1)}, f32[1,128,256]{2,1,0:T(8,128)S(1)}, u32[]{:S(2)}, u32[]{:S(2)}) collective-permute-start(f32[1,128,256]{2,1,0:T(8,128)S(1)} %get-tuple-element.22), channel_id=1, source_target_pairs={{1,0},{2,1},{3,2},{4,3},{5,4},{6,5},{7,6},{8,7},{9,8},{10,9},{11,1... | collective-permute-start | bytes 393224 | tf_op jit(solution)/shard_map/ppermute | solution.py:15
  7.5 5.9 %copy-start.17 = (f32[2,128,256]{2,1,0:T(8,128)}, f32[2,128,256]{2,1,0:T(8,128)S(1)}, u32[]{:S(2)}) copy-start(f32[2,128,256]{2,1,0:T(8,128)S(1)} %reshape.23) | copy-start | bytes 786436
  7.5 5.4 %copy-start.1 = (f32[16,2,128,256]{3,2,1,0:T(8,128)S(1)}, f32[16,2,128,256]{3,2,1,0:T(8,128)}, u32[]{:S(2)}) copy-start(f32[16,2,128,256]{3,2,1,0:T(8,128)} %param.5) | copy-start | bytes 12582916
  12.9 20.5 %copy-start.12 = (f32[2,128,256]{2,1,0:T(8,128)}, f32[2,128,256]{2,1,0:T(8,128)S(1)}, u32[]{:S(2)}) copy-start(f32[2,128,256]{2,1,0:T(8,128)S(1)} %get-tuple-element.10) | copy-start | bytes 786436
  12.9 20.5 %copy-start.14 = (f32[2,128,256]{2,1,0:T(8,128)}, f32[2,128,256]{2,1,0:T(8,128)S(1)}, u32[]{:S(2)}) copy-start(f32[2,128,256]{2,1,0:T(8,128)S(1)} %get-tuple-element.11) | copy-start | bytes 786436
  12.9 94.9 %copy-start.10 = (f32[2,128,256]{2,1,0:T(8,128)}, f32[2,128,256]{2,1,0:T(8,128)S(1)}, u32[]{:S(2)}) copy-start(f32[2,128,256]{2,1,0:T(8,128)S(1)} %get-tuple-element.9) | copy-start | bytes 786436
  13.7 9.2 %collective-permute-start.2 = (f32[16,1,128,256]{3,2,1,0:T(8,128)S(1)}, f32[16,1,128,256]{3,2,1,0:T(8,128)S(1)}, u32[]{:S(2)}, u32[]{:S(2)}) collective-permute-start(f32[16,1,128,256]{3,2,1,0:T(8,128)S(1)} %get-tuple-element.20), channel_id=1, source_target_pairs={{0,1},{1,2},{2,3},{3,4},{4,5},{5,6},{6,7},{7,8},{8,9},{9,10},{10,1... | collective-permute-start | bytes 6291464 | tf_op jit(solution)/shard_map/ppermute | solution.py:14
  19.3 14.1 %copy-start.9 = (f32[2,128,256]{2,1,0:T(8,128)S(1)}, f32[2,128,256]{2,1,0:T(8,128)}, u32[]{:S(2)}) copy-start(f32[2,128,256]{2,1,0:T(8,128)} %param.7) | copy-start | bytes 786436
  19.3 6.2 %collective-permute-start.3 = (f32[16,1,128,256]{3,2,1,0:T(8,128)S(1)}, f32[16,1,128,256]{3,2,1,0:T(8,128)S(1)}, u32[]{:S(2)}, u32[]{:S(2)}) collective-permute-start(f32[16,1,128,256]{3,2,1,0:T(8,128)S(1)} %get-tuple-element.21), channel_id=1, source_target_pairs={{1,0},{2,1},{3,2},{4,3},{5,4},{6,5},{7,6},{8,7},{9,8},{10,9},{11,1... | collective-permute-start | bytes 6291464 | tf_op jit(solution)/shard_map/ppermute | solution.py:15
  25.5 7.9 %copy-start.7 = (f32[16,1,128,256]{3,2,1,0:T(8,128)}, f32[16,1,128,256]{3,2,1,0:T(8,128)S(1)}, u32[]{:S(2)}) copy-start(f32[16,1,128,256]{3,2,1,0:T(8,128)S(1)} %collective-permute-done.3) | copy-start | bytes 6291460
  46.6 53.3 %copy-start.3 = (f32[16,2,128,256]{3,2,1,0:T(8,128)S(1)}, f32[16,2,128,256]{3,2,1,0:T(8,128)}, u32[]{:S(2)}) copy-start(f32[16,2,128,256]{3,2,1,0:T(8,128)} %fusion.51) | copy-start | bytes 12582916
  49.3 44.9 %collective-permute-start.4 = (f32[16,1,128,256]{3,2,1,0:T(8,128)S(1)}, f32[16,1,128,256]{3,2,1,0:T(8,128)S(1)}, u32[]{:S(2)}, u32[]{:S(2)}) collective-permute-start(f32[16,1,128,256]{3,2,1,0:T(8,128)S(1)} %get-tuple-element.18), channel_id=1, source_target_pairs={{0,1},{1,2},{2,3},{3,4},{4,5},{5,6},{6,7},{7,8},{8,9},{9,10},{10,1... | collective-permute-start | bytes 6291464 | tf_op jit(solution)/shard_map/ppermute | solution.py:14
  90.6 7.9 %collective-permute-start.5 = (f32[16,1,128,256]{3,2,1,0:T(8,128)S(1)}, f32[16,1,128,256]{3,2,1,0:T(8,128)S(1)}, u32[]{:S(2)}, u32[]{:S(2)}) collective-permute-start(f32[16,1,128,256]{3,2,1,0:T(8,128)S(1)} %get-tuple-element.19), channel_id=1, source_target_pairs={{1,0},{2,1},{3,2},{4,3},{5,4},{6,5},{7,6},{8,7},{9,8},{10,9},{11,1... | collective-permute-start | bytes 6291464 | tf_op jit(solution)/shard_map/ppermute | solution.py:15
  98.5 1.3 copy-start.6
  233.1 91.7 %copy-start = (f32[16,2,128,256]{3,2,1,0:T(8,128)}, f32[16,2,128,256]{3,2,1,0:T(8,128)S(1)}, u32[]{:S(2)}) copy-start(f32[16,2,128,256]{3,2,1,0:T(8,128)S(1)} %multiply_add_fusion) | copy-start | bytes 12582916
  233.6 5.5 %collective-permute-start.6 = (f32[16,1,128,256]{3,2,1,0:T(8,128)S(1)}, f32[16,1,128,256]{3,2,1,0:T(8,128)S(1)}, u32[]{:S(2)}, u32[]{:S(2)}) collective-permute-start(f32[16,1,128,256]{3,2,1,0:T(8,128)S(1)} %get-tuple-element.16), channel_id=1, source_target_pairs={{0,1},{1,2},{2,3},{3,4},{4,5},{5,6},{6,7},{7,8},{8,9},{9,10},{10,1... | collective-permute-start | bytes 6291464 | tf_op jit(solution)/shard_map/ppermute | solution.py:14
  235.5 15.5 %copy-start.11 = (f32[2,128,256]{2,1,0:T(8,128)S(1)}, f32[2,128,256]{2,1,0:T(8,128)}, u32[]{:S(2)}) copy-start(f32[2,128,256]{2,1,0:T(8,128)} %copy-done.10) | copy-start | bytes 786436
  235.5 15.5 %copy-start.13 = (f32[2,128,256]{2,1,0:T(8,128)S(1)}, f32[2,128,256]{2,1,0:T(8,128)}, u32[]{:S(2)}) copy-start(f32[2,128,256]{2,1,0:T(8,128)} %copy-done.12) | copy-start | bytes 786436
  235.5 15.5 %copy-start.15 = (f32[2,128,256]{2,1,0:T(8,128)S(1)}, f32[2,128,256]{2,1,0:T(8,128)}, u32[]{:S(2)}) copy-start(f32[2,128,256]{2,1,0:T(8,128)} %copy-done.14) | copy-start | bytes 786436
  235.5 15.5 %copy-start.16 = (f32[2,128,256]{2,1,0:T(8,128)S(1)}, f32[2,128,256]{2,1,0:T(8,128)}, u32[]{:S(2)}) copy-start(f32[2,128,256]{2,1,0:T(8,128)} %get-tuple-element.12) | copy-start | bytes 786436
  235.6 6.2 %collective-permute-start.7 = (f32[16,1,128,256]{3,2,1,0:T(8,128)S(1)}, f32[16,1,128,256]{3,2,1,0:T(8,128)S(1)}, u32[]{:S(2)}, u32[]{:S(2)}) collective-permute-start(f32[16,1,128,256]{3,2,1,0:T(8,128)S(1)} %get-tuple-element.17), channel_id=1, source_target_pairs={{1,0},{2,1},{3,2},{4,3},{5,4},{6,5},{7,6},{8,7},{9,8},{10,9},{11,1... | collective-permute-start | bytes 6291464 | tf_op jit(solution)/shard_map/ppermute | solution.py:15
  241.7 1.3 copy-start.8
  263.8 53.1 %copy-start.2 = (f32[16,2,128,256]{3,2,1,0:T(8,128)S(1)}, f32[16,2,128,256]{3,2,1,0:T(8,128)}, u32[]{:S(2)}) copy-start(f32[16,2,128,256]{3,2,1,0:T(8,128)} %fusion.22) | copy-start | bytes 12582916
  266.5 44.8 %collective-permute-start.8 = (f32[16,1,128,256]{3,2,1,0:T(8,128)S(1)}, f32[16,1,128,256]{3,2,1,0:T(8,128)S(1)}, u32[]{:S(2)}, u32[]{:S(2)}) collective-permute-start(f32[16,1,128,256]{3,2,1,0:T(8,128)S(1)} %get-tuple-element.14), channel_id=1, source_target_pairs={{0,1},{1,2},{2,3},{3,4},{4,5},{5,6},{6,7},{7,8},{8,9},{9,10},{10,1... | collective-permute-start | bytes 6291464 | tf_op jit(solution)/shard_map/ppermute | solution.py:14
  307.7 7.9 %collective-permute-start.9 = (f32[16,1,128,256]{3,2,1,0:T(8,128)S(1)}, f32[16,1,128,256]{3,2,1,0:T(8,128)S(1)}, u32[]{:S(2)}, u32[]{:S(2)}) collective-permute-start(f32[16,1,128,256]{3,2,1,0:T(8,128)S(1)} %get-tuple-element.15), channel_id=1, source_target_pairs={{1,0},{2,1},{3,2},{4,3},{5,4},{6,5},{7,6},{8,7},{9,8},{10,9},{11,1... | collective-permute-start | bytes 6291464 | tf_op jit(solution)/shard_map/ppermute | solution.py:15
  311.3 4.3 %copy-start.4 = (f32[16,1,128,256]{3,2,1,0:T(8,128)}, f32[16,1,128,256]{3,2,1,0:T(8,128)S(1)}, u32[]{:S(2)}) copy-start(f32[16,1,128,256]{3,2,1,0:T(8,128)S(1)} %collective-permute-done.8) | copy-start | bytes 6291460
  315.6 1.3 copy-start.5
  413.2 1.8 copy-start.18
where the time goes:
time: 416 us; the launch traced here: 415 us
  blocking collectives  167 us (40%)
  other arithmetic  110 us (26%)
  starting transfers between devices  99.3 us (24%)
  waiting for transfers between devices  24.1 us (6%)
  local copies, waits for them, and re-layouts  13.2 us (3%)
    psum x2, blocking collectives, norm_sum(): return lax.psum(inner(left, right), 'gx')  98.8 us
    ppermute x5, starting transfers between devices, with_halo(): before = lax.ppermute(last, axis, up)  92.2 us
    psum x1, blocking collectives, shards(): alpha = gamma / lax.psum(inner(direction, image), 'gx')  68.4 us
    reduce_sum x3, other arithmetic, inner(): return jnp.sum(first * second, axis=(1, 2, 3))  37.3 us
    concatenate x5, other arithmetic, with_halo(): shard = jnp.concatenate([before, shard, after], axis=dim)  32.9 us
    add x2, other arithmetic, apply_k(): total = total + 0.5 * (kc + kn) * (vc - vn)  25.9 us
    ppermute x5, waiting for transfers between devices, with_halo(): after = lax.ppermute(leading, axis, down)  15.5 us
    ppermute x5, waiting for transfers between devices, with_halo(): before = lax.ppermute(last, axis, up)  8.62 us
  transfers between devices with their start and end apart: 10, of which 9 were waited for; matrix products, arithmetic and copies ran while one was open for 1% of the time, Pallas kernels for 0%

commit v1 on v0

v1 whole, which is shorter than its diff:
```python
import functools

import jax
import jax.numpy as jnp
from jax import lax
from jax.experimental import pallas as pl
from jax.experimental.pallas import tpu as pltpu
from jax.sharding import PartitionSpec as P

GROUP = 4
CHUNK = 32
HIGH = lax.Precision.HIGHEST


def body(ng, sems, probes, kappa, delta, cells, weights, out, grad,
         bp, uu, tt, ww, qq, kap, dlt, kd, pre, obs, cx, cym, cyp, czm, czp,
         sc, sw, part1, part2, sum1, sum2, acc, red1, red2, relay,
         send_sem, recv_sem, local_sem):
    share = probes.shape[0] // GROUP
    rows, ny, nz = kappa.shape
    deep = GROUP * rows
    me = lax.axis_index("gx")
    g = lax.div(me, GROUP)
    j = lax.rem(me, GROUP)
    mates = {1: j + 1 - 2 * lax.rem(j, 2), 2: lax.rem(j + 2, 4), 3: 3 - j}
    has_low = g > 0
    has_high = g < ng - 1
    counter = [0]

    def remote(src, dst, target):
        k = counter[0]
        counter[0] += 1
        return pltpu.make_async_remote_copy(
            src_ref=src, dst_ref=dst, send_sem=send_sem.at[k],
            recv_sem=recv_sem.at[k], device_id={"gx": target},
            device_id_type=pl.DeviceIdType.MESH)

    barrier = pltpu.get_barrier_semaphore()
    for k in mates:
        pl.semaphore_signal(barrier, inc=1, device_id={"gx": g * GROUP + mates[k]},
                            device_id_type=pl.DeviceIdType.MESH)
    column = [lax.rem(g + d, ng) * GROUP + j for d in range(1, ng)]
    for other in column:
        pl.semaphore_signal(barrier, inc=1, device_id={"gx": other},
                            device_id_type=pl.DeviceIdType.MESH)
    pl.semaphore_wait(barrier, 3 + ng - 1)

    def mate(k):
        return g * GROUP + mates[k]

    mine_k = kap.at[pl.ds(1 + rows * j, rows)]
    mine_d = dlt.at[pl.ds(rows * j, rows)]
    direct = {}
    for k in (2, 1):
        direct[k] = [remote(kappa, mine_k, mate(k)), remote(delta, mine_d, mate(k))]
        for c in direct[k]:
            c.start()
    listed = []
    for k in (2, 3, 1):
        listed += [remote(cells, sc.at[j], mate(k)), remote(weights, sw.at[j], mate(k))]
    for c in listed:
        c.start()
    swaps = []
    for p in range(share):
        group = []
        for k in (2, 3, 1):
            c = remote(probes.at[share * mates[k] + p],
                       bp.at[p, pl.ds(rows * j, rows)], mate(k))
            c.start()
            group.append(c)
        swaps.append(group)
    own = [
        pltpu.make_async_copy(kappa, mine_k, local_sem.at[0]),
        pltpu.make_async_copy(delta, mine_d, local_sem.at[1]),
        pltpu.make_async_copy(cells, sc.at[j], local_sem.at[2]),
        pltpu.make_async_copy(weights, sw.at[j], local_sem.at[3]),
    ] + [
        pltpu.make_async_copy(probes.at[share * j + p],
                              bp.at[p, pl.ds(rows * j, rows)], local_sem.at[4 + p])
        for p in range(share)
    ]
    for c in own:
        c.start()

    class Halo:
        def __init__(self, low, first, last, high):
            self.up = remote(last, low, me + GROUP)
            self.down = remote(first, high, me - GROUP)

        def start(self):
            pl.when(has_high)(self.up.start)
            pl.when(has_low)(self.down.start)

        def wait_recv(self):
            pl.when(has_low)(self.up.wait_recv)
            pl.when(has_high)(self.down.wait_recv)

        def wait_send(self):
            pl.when(has_high)(self.up.wait_send)
            pl.when(has_low)(self.down.wait_send)

    def halo_of(field, p):
        f = field.at[p]
        return Halo(f.at[0], f.at[1], f.at[deep], f.at[deep + 1])

    zero = jnp.zeros((ny, nz), jnp.float32)

    @pl.when(g == 0)
    def _():
        kap[0] = zero
        for p in range(share):
            uu[p, 0] = zero
            tt[p, 0] = zero
            ww[p, 0] = zero

    @pl.when(g == ng - 1)
    def _():
        kap[deep + 1] = zero
        for p in range(share):
            uu[p, deep + 1] = zero
            tt[p, deep + 1] = zero
            ww[p, deep + 1] = zero

    for c in direct[2]:
        c.wait_recv()
    far_k = kap.at[pl.ds(1 + rows * mates[2], rows)]
    far_d = dlt.at[pl.ds(rows * mates[2], rows)]
    passed = [remote(far_k, far_k, mate(1)), remote(far_d, far_d, mate(1))]
    for c in passed:
        c.start()
    for c in listed:
        c.wait_recv()
    for c in own[:4]:
        c.wait()
    for k in range(GROUP):
        local = sc[k] - (g * GROUP + k) * (rows * ny * nz)
        row = lax.div(local, nz)
        col = local - row * nz
        sens = local.shape[1]
        at_row = lax.broadcasted_iota(jnp.int32, (rows * ny, sens), 0) == row
        at_col = lax.broadcasted_iota(jnp.int32, (nz, sens), 0) == col
        left = jnp.where(at_row, sw[k], 0.0)
        right = jnp.where(at_col, 1.0, 0.0)
        obs[rows * k:rows * (k + 1)] = lax.dot_general(
            left, right, (((1,), (1,)), ((), ())), precision=HIGH,
            preferred_element_type=jnp.float32).reshape(rows, ny, nz)
    for c in direct[1] + passed:
        c.wait_recv()
    edge = Halo(kap.at[0], kap.at[1], kap.at[deep], kap.at[deep + 1])
    edge.start()

    y_at = lax.broadcasted_iota(jnp.int32, (ny, nz), 0)
    z_at = lax.broadcasted_iota(jnp.int32, (ny, nz), 1)

    def faces(l, _):
        k = kap[l + 1]
        total = dlt[l]
        for ref, axis, shift, size, index, bound in (
            (cym, 0, 1, ny, y_at, 0), (cyp, 0, ny - 1, ny, y_at, ny - 1),
            (czm, 1, 1, nz, z_at, 0), (czp, 1, nz - 1, nz, z_at, nz - 1),
        ):
            near = pltpu.roll(k, shift, axis)
            f = 0.5 * (k + jnp.where(index == bound, 0.0, near))
            ref[l] = jnp.where(index == bound, 0.0, f)
            total = total + f
        kd[l] = total
        return 0

    lax.fori_loop(0, deep, faces, 0)
    edge.wait_recv()

    def across(l, _):
        cx[l] = 0.5 * (kap[l] + kap[l + 1])
        return 0

    lax.fori_loop(0, deep + 1, across, 0)

    def invert(l, _):
        d = kd[l] + cx[l] + cx[l + 1]
        kd[l] = d
        pre[l] = 1.0 / (d * d + obs[l])
        return 0

    lax.fori_loop(0, deep, invert, 0)

    chunks = [pl.ds(r, CHUNK) for r in range(0, ny, CHUNK)]

    def fold(x):
        x = x[:, :128] + x[:, 128:]
        return jnp.sum(x.reshape(CHUNK // 8, 8, 128), axis=0)

    def apply_k(field, p, l, r):
        rs = pl.ds(r, CHUNK)
        v = field[p, l + 1, rs]
        ym = pltpu.roll(v, 1, 0) if r == 0 else field[p, l + 1, pl.ds(r - 1, CHUNK)]
        yp = (pltpu.roll(v, CHUNK - 1, 0) if r + CHUNK == ny
              else field[p, l + 1, pl.ds(r + 1, CHUNK)])
        total = kd[l, rs] * v
        total = total - cx[l, rs] * field[p, l, rs]
        total = total - cx[l + 1, rs] * field[p, l + 2, rs]
        total = total - cym[l, rs] * ym
        total = total - cyp[l, rs] * yp
        total = total - czm[l, rs] * pltpu.roll(v, 1, 1)
        total = total - czp[l, rs] * pltpu.roll(v, nz - 1, 1)
        return total

    none = jnp.zeros((8, 128), jnp.float32)

    def put(ref, at, value):
        ref[at:at + 1] = jnp.sum(value, axis=0, keepdims=True)

    u_halo, t_halo, w_halo = [], [], []

    def begin(p):
        for c in swaps[p]:
            c.wait_recv()
        own[4 + p].wait()

        def layer(l, total):
            for rs in chunks:
                b = bp[p, l, rs]
                u = pre[l, rs] * b
                uu[p, l + 1, rs] = u
                total = total + fold(b * u)
            return total

        put(part1, 2 * p, lax.fori_loop(0, deep, layer, none))
        h = halo_of(uu, p)
        h.start()
        u_halo.append(h)

    def first(p):
        u_halo[p].wait_recv()

        def layer(l, total):
            for r in range(0, ny, CHUNK):
                rs = pl.ds(r, CHUNK)
                t = apply_k(uu, p, l, r)
                tt[p, l + 1, rs] = t
                u = uu[p, l + 1, rs]
                total = total + fold(t * t + obs[l, rs] * u * u)
            return total

        put(part1, 2 * p + 1, lax.fori_loop(0, deep, layer, none))
        h = halo_of(tt, p)
        h.start()
        t_halo.append(h)

    def second(p):
        t_halo[p].wait_recv()

        def layer(l, _):
            for r in range(0, ny, CHUNK):
                rs = pl.ds(r, CHUNK)
                q = apply_k(tt, p, l, r) + obs[l, rs] * uu[p, l + 1, rs]
                qq[p, l, rs] = q
                ww[p, l + 1, rs] = pre[l, rs] * q
            return 0

        lax.fori_loop(0, deep, layer, 0)
        h = halo_of(ww, p)
        h.start()
        w_halo.append(h)

    def share_sum(part, slots):
        sent = [remote(part, slots.at[g], other) for other in column]
        for c in sent:
            c.start()
        slots[g] = part[...]
        return sent

    def total_of(sent, slots):
        for c in sent:
            c.wait_recv()
        total = slots[0]
        for k in range(1, ng):
            total = total + slots[k]
        return jnp.sum(total, axis=1, keepdims=True)

    for i in range(share + 2):
        if i < share:
            begin(i)
        if 1 <= i <= share:
            first(i - 1)
        if i == share:
            sent1 = share_sum(part1, sum1)
        if i >= 2:
            second(i - 2)
    sums = total_of(sent1, sum1)
    gamma = [sums[2 * p:2 * p + 1] for p in range(share)]
    curve = [sums[2 * p + 1:2 * p + 2] for p in range(share)]
    alpha = [gamma[p] / curve[p] for p in range(share)]
    for p in range(share):
        w_halo[p].wait_recv()
        a = alpha[p]

        def layer(l, totals):
            s_sum, e_sum, g_sum = totals
            for r in range(0, ny, CHUNK):
                rs = pl.ds(r, CHUNK)
                s = tt[p, l + 1, rs] - a * apply_k(ww, p, l, r)
                q = qq[p, l, rs]
                u = uu[p, l + 1, rs] - a * ww[p, l + 1, rs]
                resid = bp[p, l, rs] - a * q
                s_sum = s_sum + fold(s * s + obs[l, rs] * u * u)
                e_sum = e_sum + fold(u * q)
                g_sum = g_sum + fold(resid * u)
            return s_sum, e_sum, g_sum

        found = lax.fori_loop(0, deep, layer, (none, none, none))
        for k in range(3):
            put(part2, 4 * p + k, found[k])
        part2[4 * p + 3:4 * p + 4] = jnp.zeros((1, 128), jnp.float32)
    sent2 = share_sum(part2, sum2)
    sums = total_of(sent2, sum2)
    on_u, on_w = [], []
    for p in range(share):
        d2, e2, g2 = (sums[4 * p + k:4 * p + k + 1] for k in range(3))
        beta = g2 / gamma[p]
        step = g2 / (d2 + 2.0 * beta * e2 + beta * beta * curve[p])
        on_u.append(alpha[p] + step * (1.0 + beta))
        on_w.append(alpha[p] * step)

    def estimate(l, _):
        for rs in chunks:
            total = jnp.zeros((CHUNK, nz), jnp.float32)
            for p in range(share):
                x = on_u[p] * uu[p, l + 1, rs] - on_w[p] * ww[p, l + 1, rs]
                total = total + bp[p, l, rs] * x
            acc[l, rs] = total
        return 0

    lax.fori_loop(0, deep, estimate, 0)
    near = [remote(acc.at[pl.ds(rows * mates[3], rows)], red1.at[1], mate(1)),
            remote(acc.at[pl.ds(rows * mates[1], rows)], red1.at[0], mate(1))]
    for c in near:
        c.start()
    near[0].wait_recv()
    relay[...] = acc[pl.ds(rows * mates[2], rows)] + red1[1]
    across_y = remote(relay, red2, mate(2))
    across_y.start()
    near[1].wait_recv()
    partial = acc[pl.ds(rows * j, rows)] + red1[0]
    across_y.wait_recv()
    diag = (partial + red2[...]) * (0.5 / probes.shape[0])
    out[...] = diag

    local = cells[...] - me * (rows * ny * nz)
    row = lax.div(local, nz)
    col = local - row * nz
    sens = local.shape[1]
    at_row = lax.broadcasted_iota(jnp.int32, (rows * ny, sens), 0) == row
    at_col = lax.broadcasted_iota(jnp.int32, (nz, sens), 0) == col
    picked = lax.dot_general(
        diag.reshape(rows * ny, nz), jnp.where(at_col, 1.0, 0.0),
        (((1,), (0,)), ((), ())), precision=HIGH, preferred_element_type=jnp.float32)
    grad[...] = jnp.sum(jnp.where(at_row, picked, 0.0), axis=0, keepdims=True)

    for c in direct[1] + direct[2] + listed + passed + near + [across_y] + sent1 + sent2:
        c.wait_send()
    for group in swaps:
        for c in group:
            c.wait_send()
    for h in [edge] + u_halo + t_halo + w_halo:
        h.wait_send()
    assert counter[0] == sems


def shards(probes, kappa, delta, sensor_cells, sensor_weights):
    count, rows, ny, nz = probes.shape
    ng = lax.axis_size("gx") // GROUP
    share, deep = count // GROUP, GROUP * rows
    sens = sensor_cells.shape[0]
    sems = 4 + 6 + 3 * share + 2 + 2 + 6 * share + 2 * (ng - 1) + 3
    f32 = jnp.float32
    field = pltpu.VMEM((deep, ny, nz), f32)
    padded = pltpu.VMEM((share, deep + 2, ny, nz), f32)
    plain = pltpu.VMEM((share, deep, ny, nz), f32)
    any_ = pl.BlockSpec(memory_space=pl.ANY)
    vmem = pl.BlockSpec(memory_space=pltpu.VMEM)
    diag, grad = pl.pallas_call(
        functools.partial(body, ng, sems),
        out_shape=(jax.ShapeDtypeStruct((rows, ny, nz), f32),
                   jax.ShapeDtypeStruct((1, sens), f32)),
        in_specs=[any_, any_, any_, vmem, vmem],
        out_specs=(vmem, vmem),
        scratch_shapes=[
            plain, padded, padded, padded, plain,
            pltpu.VMEM((deep + 2, ny, nz), f32), field, field, field, field,
            pltpu.VMEM((deep + 1, ny, nz), f32), field, field, field, field,
            pltpu.VMEM((GROUP, 1, sens), jnp.int32),
            pltpu.VMEM((GROUP, 1, sens), f32),
            pltpu.VMEM((2 * share, 128), f32),
            pltpu.VMEM((4 * share, 128), f32),
            pltpu.VMEM((ng, 2 * share, 128), f32),
            pltpu.VMEM((ng, 4 * share, 128), f32),
            field,
            pltpu.VMEM((2, rows, ny, nz), f32),
            pltpu.VMEM((rows, ny, nz), f32),
            pltpu.VMEM((rows, ny, nz), f32),
            pltpu.SemaphoreType.DMA((sems,)),
            pltpu.SemaphoreType.DMA((sems,)),
            pltpu.SemaphoreType.DMA((4 + share,)),
        ],
        compiler_params=pltpu.CompilerParams(
            collective_id=0, has_side_effects=True,
            vmem_limit_bytes=52 * 1024 * 1024),
        cost_estimate=pl.CostEstimate(
            flops=100 * probes.size, bytes_accessed=6 * probes.size, transcendentals=0),
    )(probes, kappa, delta, sensor_cells.reshape(1, sens), sensor_weights.reshape(1, sens))
    return diag, grad.reshape(sens)


def solution(mesh):
    placed = (
        P("grp", "gx", None, None),
        P(("grp", "gx"), None, None),
        P(("grp", "gx"), None, None),
        P(("grp", "gx")),
        P(("grp", "gx")),
    )
    return jax.shard_map(
        shards,
        mesh=mesh,
        in_specs=placed,
        out_specs=(P(("grp", "gx"), None, None), P(("grp", "gx"))),
        check_vma=False,
    )
```

time: 416 us -> 102 us (0.25)
  blocking collectives: 167 us -> 0 us
  other arithmetic: 110 us -> 0 us
  starting transfers between devices: 99.3 us -> 0 us
  Pallas kernels: 0 us -> 96.8 us
  waiting for transfers between devices: 24.1 us -> 0 us
  local copies, waits for them, and re-layouts: 13.2 us -> 4.42 us
    psum x3 -> x0, blocking collectives: 167 us -> none  [the longest x2 98.8 us: norm_sum(): return lax.psum(inner(left, right), 'gx')]
    ppermute x10 -> x0, starting transfers between devices: 99.3 us -> none  [the longest x5 92.2 us: with_halo(): before = lax.ppermute(last, axis, up)]
    pallas_call x0 -> x1, Pallas kernels: none -> 96.8 us  [shards(): pl.pallas_call(functools.partial(body, ng, sems), out_shape=(jax.ShapeDty...]
    reduce_sum x4 -> x0, other arithmetic: 41.9 us -> none  [the longest x3 37.3 us: inner(): return jnp.sum(first * second, axis=(1, 2, 3))]
    concatenate x5 -> x0, other arithmetic: 32.9 us -> none  [with_halo(): shard = jnp.concatenate([before, shard, after], axis=dim)]
    add x3 -> x0, other arithmetic: 30.4 us -> none  [the longest x2 25.9 us: apply_k(): total = total + 0.5 * (kc + kn) * (vc - vn)]
    ppermute x10 -> x0, waiting for transfers between devices: 24.1 us -> none  [the longest x5 15.5 us: with_halo(): after = lax.ppermute(leading, axis, down)]
    slice x5 -> x0, local copies, waits for them, and re-layouts: 7.19 us -> none  [the longest x4 6.2 us: with_halo(): last = lax.slice_in_dim(shard, length - width, length, axis=dim)]
  transfers between devices with their start and end apart: 10 -> 0, of which waited for: 9 -> 0; matrix products, arithmetic and copies ran while one was open for 1% -> 0% of each run, Pallas kernels for 0% -> 0%
where the time goes in v1:
time: 102 us
  Pallas kernels  96.8 us (95%)
  local copies, waits for them, and re-layouts  4.42 us (4%)
    pallas_call x1, Pallas kernels, shards(): pl.pallas_call(functools.partial(body, ng, sems), out_shape=(jax.ShapeDty...  96.8 us
    unnamed x10, local copies, waits for them, and re-layouts  4.42 us

profile of v1, /device:TPU:0, one launch (start us, length us, event | category | flops | bytes accessed | tf_op | source)
XLA Modules:
  0.0 101.9 jit_solution(10596897889525711545)
XLA Ops:
  0.6 0.0 copy-start
  0.6 0.9 copy-done
  1.6 0.0 copy-start.1
  1.6 0.9 copy-done.1
  2.5 0.0 copy-start.2
  2.5 0.7 copy-done.2
  3.2 0.0 copy-start.3
  3.2 0.7 copy-done.3
  3.8 96.8 %shard_map.68 = (f32[2,128,256]{2,1,0:T(8,128)S(1)}, f32[1,128]{1,0:T(1,128)S(1)}) custom-call(f32[16,2,128,256]{3,2,1,0:T(8,128)} %probes.1, f32[2,128,256]{2,1,0:T(8,128)S(1)} %copy-done, f32[2,128,256]{2,1,0:T(8,128)S(1)} %copy-done.1, s32[1,128]{1,0:T(1,128)S(1)} %bitcast.3, f32[1,128]{1,0:T(1,128)S(1)} %bitcast.4), custom_call_target="tpu_custom_call" | custom-call | flops 104857600 | bytes 6291456 | tf_op jit(solution)/shard_map/pallas_call | solution.py:381
  100.7 0.7 copy.9
  101.4 0.5 copy.10
Async XLA Ops:
  0.6 1.0 copy-start
  1.6 0.9 copy-start.1
  2.5 0.7 copy-start.2
  3.2 0.7 copy-start.3

commit v2 on v1

--- a/solution.py
+++ b/solution.py
@@ -61,14 +61,16 @@
     for c in listed:
         c.start()
     swaps = []
-    for p in range(share):
-        group = []
-        for k in (2, 3, 1):
-            c = remote(probes.at[share * mates[k] + p],
-                       bp.at[p, pl.ds(rows * j, rows)], mate(k))
-            c.start()
-            group.append(c)
-        swaps.append(group)
+    edge_row = lax.div(j, 2)
+    for row in (edge_row, 1 - edge_row):
+        for p in range(share):
+            group = []
+            for k in (2, 3, 1):
+                c = remote(probes.at[share * mates[k] + p, pl.ds(row, 1)],
+                           bp.at[p, pl.ds(rows * j + row, 1)], mate(k))
+                c.start()
+                group.append(c)
+            swaps.append(group)
     own = [
         pltpu.make_async_copy(kappa, mine_k, local_sem.at[0]),
         pltpu.make_async_copy(delta, mine_d, local_sem.at[1]),
@@ -209,39 +211,44 @@
     def put(ref, at, value):
         ref[at:at + 1] = jnp.sum(value, axis=0, keepdims=True)
 
-    u_halo, t_halo, w_halo = [], [], []
-
-    def begin(p):
+    u_halo, t_halo, w_halo, sent1 = [], [], [], []
+
+    def border(p):
         for c in swaps[p]:
             c.wait_recv()
         own[4 + p].wait()
-
-        def layer(l, total):
-            for rs in chunks:
-                b = bp[p, l, rs]
-                u = pre[l, rs] * b
-                uu[p, l + 1, rs] = u
-                total = total + fold(b * u)
-            return total
-
-        put(part1, 2 * p, lax.fori_loop(0, deep, layer, none))
+        uu[p, 1] = pre[0] * bp[p, 0]
+        uu[p, deep] = pre[deep - 1] * bp[p, deep - 1]
         h = halo_of(uu, p)
         h.start()
         u_halo.append(h)
 
     def first(p):
+        for c in swaps[share + p]:
+            c.wait_recv()
+
+        def scale(l, _):
+            uu[p, l + 1] = pre[l] * bp[p, l]
+            return 0
+
+        lax.fori_loop(1, deep - 1, scale, 0)
         u_halo[p].wait_recv()
 
-        def layer(l, total):
+        def layer(l, totals):
+            g_sum, c_sum = totals
             for r in range(0, ny, CHUNK):
                 rs = pl.ds(r, CHUNK)
                 t = apply_k(uu, p, l, r)
                 tt[p, l + 1, rs] = t
                 u = uu[p, l + 1, rs]
-                total = total + fold(t * t + obs[l, rs] * u * u)
-            return total
-
-        put(part1, 2 * p + 1, lax.fori_loop(0, deep, layer, none))
+                g_sum = g_sum + fold(bp[p, l, rs] * u)
+                c_sum = c_sum + fold(t * t + obs[l, rs] * u * u)
+            return g_sum, c_sum
+
+        found = lax.fori_loop(0, deep, layer, (none, none))
+        for k in range(2):
+            put(part1.at[p], k, found[k])
+        sent1.append(share_sum(part1.at[p], sum1.at[p]))
         h = halo_of(tt, p)
         h.start()
         t_halo.append(h)
@@ -277,22 +284,15 @@
             total = total + slots[k]
         return jnp.sum(total, axis=1, keepdims=True)
 
-    for i in range(share + 2):
-        if i < share:
-            begin(i)
-        if 1 <= i <= share:
-            first(i - 1)
-        if i == share:
-            sent1 = share_sum(part1, sum1)
-        if i >= 2:
-            second(i - 2)
-    sums = total_of(sent1, sum1)
-    gamma = [sums[2 * p:2 * p + 1] for p in range(share)]
-    curve = [sums[2 * p + 1:2 * p + 2] for p in range(share)]
-    alpha = [gamma[p] / curve[p] for p in range(share)]
-    for p in range(share):
+    gamma, curve, alpha = [], [], []
+
+    def third(p):
+        sums = total_of(sent1[p], sum1.at[p])
+        gamma.append(sums[0:1])
+        curve.append(sums[1:2])
+        a = gamma[p] / curve[p]
+        alpha.append(a)
         w_halo[p].wait_recv()
-        a = alpha[p]
 
         def layer(l, totals):
             s_sum, e_sum, g_sum = totals
@@ -311,6 +311,18 @@
         for k in range(3):
             put(part2, 4 * p + k, found[k])
         part2[4 * p + 3:4 * p + 4] = jnp.zeros((1, 128), jnp.float32)
+
+    for p in range(share):
+        border(p)
+    for i in range(share):
+        first(i)
+        if 1 <= i:
+            second(i - 1)
+        if 2 <= i:
+            third(i - 2)
+    second(share - 1)
+    third(share - 2)
+    third(share - 1)
     sent2 = share_sum(part2, sum2)
     sums = total_of(sent2, sum2)
     on_u, on_w = [], []
@@ -330,22 +342,28 @@
             acc[l, rs] = total
         return 0
 
-    lax.fori_loop(0, deep, estimate, 0)
+    def block(at):
+        lax.fori_loop(rows * at, rows * at + rows, estimate, 0)
+
+    block(mates[3])
     near = [remote(acc.at[pl.ds(rows * mates[3], rows)], red1.at[1], mate(1)),
             remote(acc.at[pl.ds(rows * mates[1], rows)], red1.at[0], mate(1))]
-    for c in near:
-        c.start()
+    near[0].start()
+    block(mates[2])
     near[0].wait_recv()
     relay[...] = acc[pl.ds(rows * mates[2], rows)] + red1[1]
     across_y = remote(relay, red2, mate(2))
     across_y.start()
+    block(mates[1])
+    near[1].start()
+    block(j)
     near[1].wait_recv()
     partial = acc[pl.ds(rows * j, rows)] + red1[0]
     across_y.wait_recv()
     diag = (partial + red2[...]) * (0.5 / probes.shape[0])
     out[...] = diag
 
-    local = cells[...] - me * (rows * ny * nz)
+    local = sc[j] - me * (rows * ny * nz)
     row = lax.div(local, nz)
     col = local - row * nz
     sens = local.shape[1]
@@ -356,7 +374,7 @@
         (((1,), (0,)), ((), ())), precision=HIGH, preferred_element_type=jnp.float32)
     grad[...] = jnp.sum(jnp.where(at_row, picked, 0.0), axis=0, keepdims=True)
 
-    for c in direct[1] + direct[2] + listed + passed + near + [across_y] + sent1 + sent2:
+    for c in direct[1] + direct[2] + listed + passed + near + [across_y] + sum(sent1, sent2):
         c.wait_send()
     for group in swaps:
         for c in group:
@@ -371,7 +389,7 @@
     ng = lax.axis_size("gx") // GROUP
     share, deep = count // GROUP, GROUP * rows
     sens = sensor_cells.shape[0]
-    sems = 4 + 6 + 3 * share + 2 + 2 + 6 * share + 2 * (ng - 1) + 3
+    sems = 4 + 6 + 6 * share + 2 + 2 + 6 * share + (share + 1) * (ng - 1) + 3
     f32 = jnp.float32
     field = pltpu.VMEM((deep, ny, nz), f32)
     padded = pltpu.VMEM((share, deep + 2, ny, nz), f32)
@@ -382,7 +400,7 @@
         functools.partial(body, ng, sems),
         out_shape=(jax.ShapeDtypeStruct((rows, ny, nz), f32),
                    jax.ShapeDtypeStruct((1, sens), f32)),
-        in_specs=[any_, any_, any_, vmem, vmem],
+        in_specs=[any_] * 5,
         out_specs=(vmem, vmem),
         scratch_shapes=[
             plain, padded, padded, padded, plain,
@@ -390,9 +408,9 @@
             pltpu.VMEM((deep + 1, ny, nz), f32), field, field, field, field,
             pltpu.VMEM((GROUP, 1, sens), jnp.int32),
             pltpu.VMEM((GROUP, 1, sens), f32),
-            pltpu.VMEM((2 * share, 128), f32),
+            pltpu.VMEM((share, 2, 128), f32),
             pltpu.VMEM((4 * share, 128), f32),
-            pltpu.VMEM((ng, 2 * share, 128), f32),
+            pltpu.VMEM((share, ng, 2, 128), f32),
             pltpu.VMEM((ng, 4 * share, 128), f32),
             field,
             pltpu.VMEM((2, rows, ny, nz), f32),
@@ -404,7 +422,7 @@
         ],
         compiler_params=pltpu.CompilerParams(
             collective_id=0, has_side_effects=True,
-            vmem_limit_bytes=52 * 1024 * 1024),
+            vmem_limit_bytes=60 * 1024 * 1024),
         cost_estimate=pl.CostEstimate(
             flops=100 * probes.size, bytes_accessed=6 * probes.size, transcendentals=0),
     )(probes, kappa, delta, sensor_cells.reshape(1, sens), sensor_weights.reshape(1, sens))

time: 102 us -> 95.2 us (0.933)
  Pallas kernels: 96.8 us -> 91.6 us
  local copies, waits for them, and re-layouts: 4.42 us -> 2.8 us
    pallas_call x1, Pallas kernels: 96.8 us -> 91.6 us  [shards(): pl.pallas_call(functools.partial(body, ng, sems), out_shape=(jax.ShapeDty...]
    unnamed x10 -> x2, local copies, waits for them, and re-layouts: 4.42 us -> 2.8 us
where the time goes in v2:
time: 95.2 us; the launch traced here: 95.1 us
  Pallas kernels  91.6 us (96%)
  local copies, waits for them, and re-layouts  2.8 us (3%)
    pallas_call x1, Pallas kernels, shards(): pl.pallas_call(functools.partial(body, ng, sems), out_shape=(jax.ShapeDty...  91.6 us
    unnamed x2, local copies, waits for them, and re-layouts  2.8 us

profile of v2, /device:TPU:0, one launch (start us, length us, event | category | flops | bytes accessed | tf_op | source)
XLA Modules:
  0.0 95.1 jit_solution(9203546497890297518)
XLA Ops:
  0.6 91.6 %shard_map.68 = (f32[2,128,256]{2,1,0:T(8,128)}, f32[1,128]{1,0:T(1,128)}) custom-call(f32[16,2,128,256]{3,2,1,0:T(8,128)} %probes.1, f32[2,128,256]{2,1,0:T(8,128)} %kappa.1, f32[2,128,256]{2,1,0:T(8,128)} %delta.1, s32[1,128]{1,0:T(1,128)} %bitcast.3, f32[1,128]{1,0:T(1,128)} %bitcast.4), custom_call_target="tpu_custom_call" | custom-call | flops 104857600 | bytes 6291456 | tf_op jit(solution)/shard_map/pallas_call | solution.py:399
  92.3 1.7 %copy.9 = f32[2,128,256]{2,1,0:T(8,128)} copy(f32[2,128,256]{2,1,0:T(8,128)} %get-tuple-element.8) | data formatting | bytes 524288
  93.9 1.1 %copy.10 = f32[128]{0:T(128)} copy(f32[128]{0:T(128)} %bitcast.5) | data formatting | bytes 1024

commit v3 on v2

--- a/solution.py
+++ b/solution.py
@@ -245,17 +245,16 @@
                 c_sum = c_sum + fold(t * t + obs[l, rs] * u * u)
             return g_sum, c_sum
 
-        found = lax.fori_loop(0, deep, layer, (none, none))
+        found = layer(deep - 1, layer(0, (none, none)))
+        h = halo_of(tt, p)
+        h.start()
+        t_halo.append(h)
+        found = lax.fori_loop(1, deep - 1, layer, found)
         for k in range(2):
             put(part1.at[p], k, found[k])
         sent1.append(share_sum(part1.at[p], sum1.at[p]))
-        h = halo_of(tt, p)
-        h.start()
-        t_halo.append(h)
 
     def second(p):
-        t_halo[p].wait_recv()
-
         def layer(l, _):
             for r in range(0, ny, CHUNK):
                 rs = pl.ds(r, CHUNK)
@@ -264,7 +263,10 @@
                 ww[p, l + 1, rs] = pre[l, rs] * q
             return 0
 
-        lax.fori_loop(0, deep, layer, 0)
+        lax.fori_loop(1, deep - 1, layer, 0)
+        t_halo[p].wait_recv()
+        layer(0, 0)
+        layer(deep - 1, 0)
         h = halo_of(ww, p)
         h.start()
         w_halo.append(h)
@@ -292,7 +294,6 @@
         curve.append(sums[1:2])
         a = gamma[p] / curve[p]
         alpha.append(a)
-        w_halo[p].wait_recv()
 
         def layer(l, totals):
             s_sum, e_sum, g_sum = totals
@@ -307,7 +308,9 @@
                 g_sum = g_sum + fold(resid * u)
             return s_sum, e_sum, g_sum
 
-        found = lax.fori_loop(0, deep, layer, (none, none, none))
+        found = lax.fori_loop(1, deep - 1, layer, (none, none, none))
+        w_halo[p].wait_recv()
+        found = layer(deep - 1, layer(0, found))
         for k in range(3):
             put(part2, 4 * p + k, found[k])
         part2[4 * p + 3:4 * p + 4] = jnp.zeros((1, 128), jnp.float32)
@@ -342,39 +345,54 @@
             acc[l, rs] = total
         return 0
 
-    def block(at):
-        lax.fori_loop(rows * at, rows * at + rows, estimate, 0)
-
-    block(mates[3])
-    near = [remote(acc.at[pl.ds(rows * mates[3], rows)], red1.at[1], mate(1)),
-            remote(acc.at[pl.ds(rows * mates[1], rows)], red1.at[0], mate(1))]
-    near[0].start()
-    block(mates[2])
-    near[0].wait_recv()
-    relay[...] = acc[pl.ds(rows * mates[2], rows)] + red1[1]
-    across_y = remote(relay, red2, mate(2))
-    across_y.start()
-    block(mates[1])
-    near[1].start()
-    block(j)
-    near[1].wait_recv()
-    partial = acc[pl.ds(rows * j, rows)] + red1[0]
-    across_y.wait_recv()
-    diag = (partial + red2[...]) * (0.5 / probes.shape[0])
-    out[...] = diag
+    def slab(at):
+        return [rows * at + i for i in range(rows)]
+
+    def one(ref, at):
+        return ref.at[pl.ds(at, 1)]
+
+    far, near, across_y = [], [], []
+    for i, at in enumerate(slab(mates[3])):
+        estimate(at, 0)
+        c = remote(one(acc, at), one(red1.at[1], i), mate(1))
+        c.start()
+        far.append(c)
+    for i, at in enumerate(slab(mates[2])):
+        estimate(at, 0)
+        far[i].wait_recv()
+        relay[i] = acc[at] + red1[1, i]
+        c = remote(one(relay, i), one(red2, i), mate(2))
+        c.start()
+        across_y.append(c)
+    for i, at in enumerate(slab(mates[1])):
+        estimate(at, 0)
+        c = remote(one(acc, at), one(red1.at[0], i), mate(1))
+        c.start()
+        near.append(c)
+    for at in slab(j):
+        estimate(at, 0)
 
     local = sc[j] - me * (rows * ny * nz)
     row = lax.div(local, nz)
     col = local - row * nz
     sens = local.shape[1]
-    at_row = lax.broadcasted_iota(jnp.int32, (rows * ny, sens), 0) == row
+    y_row = lax.broadcasted_iota(jnp.int32, (ny, sens), 0)
     at_col = lax.broadcasted_iota(jnp.int32, (nz, sens), 0) == col
-    picked = lax.dot_general(
-        diag.reshape(rows * ny, nz), jnp.where(at_col, 1.0, 0.0),
-        (((1,), (0,)), ((), ())), precision=HIGH, preferred_element_type=jnp.float32)
-    grad[...] = jnp.sum(jnp.where(at_row, picked, 0.0), axis=0, keepdims=True)
-
-    for c in direct[1] + direct[2] + listed + passed + near + [across_y] + sum(sent1, sent2):
+    hot = jnp.where(at_col, 1.0, 0.0)
+    for i, at in enumerate(slab(j)):
+        near[i].wait_recv()
+        partial = acc[at] + red1[0, i]
+        across_y[i].wait_recv()
+        diag = (partial + red2[i]) * (0.5 / probes.shape[0])
+        out[i] = diag
+        picked = lax.dot_general(
+            diag, hot, (((1,), (0,)), ((), ())), precision=HIGH,
+            preferred_element_type=jnp.float32)
+        found = jnp.sum(jnp.where(y_row + i * ny == row, picked, 0.0),
+                        axis=0, keepdims=True)
+        grad[...] = found if i == 0 else grad[...] + found
+
+    for c in direct[1] + direct[2] + listed + passed + far + near + across_y + sum(sent1, sent2):
         c.wait_send()
     for group in swaps:
         for c in group:
@@ -389,7 +407,7 @@
     ng = lax.axis_size("gx") // GROUP
     share, deep = count // GROUP, GROUP * rows
     sens = sensor_cells.shape[0]
-    sems = 4 + 6 + 6 * share + 2 + 2 + 6 * share + (share + 1) * (ng - 1) + 3
+    sems = 4 + 6 + 6 * share + 2 + 2 + 6 * share + (share + 1) * (ng - 1) + 3 * rows
     f32 = jnp.float32
     field = pltpu.VMEM((deep, ny, nz), f32)
     padded = pltpu.VMEM((share, deep + 2, ny, nz), f32)

time: 95.2 us -> 92 us (0.966)
  Pallas kernels: 91.6 us -> 88.4 us
    pallas_call x1, Pallas kernels: 91.6 us -> 88.4 us  [shards(): pl.pallas_call(functools.partial(body, ng, sems), out_shape=(jax.ShapeDty...]
where the time goes in v3:
time: 92 us; the launch traced here: 91.9 us
  Pallas kernels  88.4 us (96%)
  local copies, waits for them, and re-layouts  2.8 us (3%)
    pallas_call x1, Pallas kernels, shards(): pl.pallas_call(functools.partial(body, ng, sems), out_shape=(jax.ShapeDty...  88.4 us
    unnamed x2, local copies, waits for them, and re-layouts  2.8 us

profile of v3, /device:TPU:0, one launch (start us, length us, event | category | flops | bytes accessed | tf_op | source)
XLA Modules:
  0.0 91.9 jit_solution(6300576436954696062)
XLA Ops:
  0.6 88.4 %shard_map.68 = (f32[2,128,256]{2,1,0:T(8,128)}, f32[1,128]{1,0:T(1,128)}) custom-call(f32[16,2,128,256]{3,2,1,0:T(8,128)} %probes.1, f32[2,128,256]{2,1,0:T(8,128)} %kappa.1, f32[2,128,256]{2,1,0:T(8,128)} %delta.1, s32[1,128]{1,0:T(1,128)} %bitcast.3, f32[1,128]{1,0:T(1,128)} %bitcast.4), custom_call_target="tpu_custom_call" | custom-call | flops 104857600 | bytes 6291456 | tf_op jit(solution)/shard_map/pallas_call | solution.py:417
  89.1 1.7 %copy.9 = f32[2,128,256]{2,1,0:T(8,128)} copy(f32[2,128,256]{2,1,0:T(8,128)} %get-tuple-element.8) | data formatting | bytes 524288
  90.7 1.1 %copy.10 = f32[128]{0:T(128)} copy(f32[128]{0:T(128)} %bitcast.5) | data formatting | bytes 1024
